TPU v7x, 512 devices: a whole 4x8x8 slice. The times are simulated.
512 devices in a mesh: patch: 4 (over x), curve: 128 (over z, y, core).
Axes of the slice: x: 4, y: 8, z: 8, core: 2. Of those that a mesh axis runs over, the one named last changes fastest.
Arguments:
- points: bfloat16 [128, 4, 256, 512], P('curve', 'patch'), may hold values from -6 to 6
- norm_gain_one: float32 [512], replicated, may hold values from 0.4 to 2.5, as said below
- qkv_one: bfloat16 [512, 1536], replicated, may hold values from -0.25 to 0.25
- out_one: bfloat16 [512, 512], replicated, may hold values from -0.25 to 0.25
- hilbert_pos: int32 [128, 4, 256], P('curve', 'patch'), may hold values from 0 to 32767, as said below
- norm_gain_two: float32 [512], replicated, may hold values from 0.4 to 2.5, as said below
- qkv_two: bfloat16 [512, 1536], replicated, may hold values from -0.25 to 0.25
- out_two: bfloat16 [512, 512], replicated, may hold values from -0.25 to 0.25
- hilbert_seg: int32 [4, 128, 256], P('patch', 'curve'), may hold values from 0 to 7, never falling along the last dimension, each value on 1 to 128 neighbouring positions
- out_grad: bfloat16 [4, 128, 256, 512], P('patch', 'curve'), may hold values from -6 to 6
Outputs:
- point_grad: bfloat16 [128, 4, 256, 512], P('curve', 'patch')
Inputs may be any that keep to these rules, and one draw needn't show every extreme that they name: `hilbert_pos`: for each index p of the second dimension, the values over all c and i form a permutation of 0 to 32767. From the points of one device at most 4 have q // 256 equal to any one value, and in every draw some device sends exactly 4 to some owner. `hilbert_seg`: within one device's slots the numbers never fall; a patch holds at most 128 slots. `norm_gain_one`: positive gains. `norm_gain_two`: positive gains.
All inputs are finite; a program needn't handle non-finite values.
Results may differ from a plain program's by a relative error of at most 0.02.
Values may be sent and summed in bfloat16 or wider, within the bound.
A program may use at most 64 MiB of HBM per device.

v0:
```python
import jax
import jax.numpy as jnp
from jax import lax
from jax.sharding import PartitionSpec as P

HEADS = 16
EPS = 1e-06


def prepare(source_rows, gain, w_qkv):
    wide = source_rows.astype(jnp.float32)
    power = jnp.mean(wide * wide, axis=-1, keepdims=True)
    normed = (wide * lax.rsqrt(power + EPS) * gain).astype(jnp.bfloat16)
    return jnp.dot(normed, w_qkv, preferred_element_type=jnp.float32).astype(jnp.bfloat16)


def finish(source_rows, mixed, w_out):
    total = source_rows.astype(jnp.float32) + jnp.dot(
        mixed, w_out, preferred_element_type=jnp.float32
    )
    return total.astype(jnp.bfloat16)


def attend(queries, keys, values, allowed):
    count, width = queries.shape
    depth = width // HEADS
    q_heads = queries.astype(jnp.float32).reshape(count, HEADS, depth)
    k_heads = keys.astype(jnp.float32).reshape(-1, HEADS, depth)
    v_heads = values.astype(jnp.float32).reshape(-1, HEADS, depth)
    scores = jnp.einsum("rhe,khe->hrk", q_heads, k_heads) * depth ** (-0.5)
    scores = jnp.where(allowed[None], scores, -1e30)
    weights = jax.nn.softmax(scores, axis=-1)
    rounded = lax.optimization_barrier(weights.astype(jnp.bfloat16))
    mixed = jnp.einsum("hrk,khe->rhe", rounded.astype(jnp.float32), v_heads)
    return mixed.reshape(count, width).astype(jnp.bfloat16)


def device_block(source_rows, segment, gain, w_qkv, w_out):
    width = source_rows.shape[1]
    packed = prepare(source_rows, gain, w_qkv)
    allowed = segment[:, None] == segment[None, :]
    mixed = attend(packed[:, :width], packed[:, width : 2 * width], packed[:, 2 * width :], allowed)
    return finish(source_rows, mixed, w_out)


def head_view(matrix, index, block, depth):
    columns = block * depth
    piece = lax.dynamic_slice_in_dim(matrix, index * columns, columns, 1)
    return piece.reshape(matrix.shape[0], block, depth)


def regroup(stacked):
    groups, length, columns = stacked.shape
    return jnp.transpose(stacked, (1, 0, 2)).reshape(length, groups * columns)


def round_trip(values):
    return lax.optimization_barrier(values.astype(jnp.bfloat16)).astype(jnp.float32)


def shards(
    points,
    norm_gain_one,
    qkv_one,
    out_one,
    hilbert_pos,
    norm_gain_two,
    qkv_two,
    out_two,
    hilbert_seg,
    out_grad,
):
    count = points.shape[2]
    width = points.shape[3]
    depth = width // HEADS
    block = 4
    groups = HEADS // block
    scale = depth ** (-0.5)
    source_rows = points.reshape(count, width)
    packed, prep_pull = jax.vjp(lambda inputs: prepare(inputs, norm_gain_one, qkv_one), source_rows)
    queries = packed[:, :width]
    gathered = lax.all_gather(packed[:, width:], "patch", axis=0, tiled=True)
    keys_all = gathered[:, :width]
    values_all = gathered[:, width:]
    patch_len = gathered.shape[0]

    def forward_group(index):
        q_part = head_view(queries, index, block, depth)
        k_part = head_view(keys_all, index, block, depth)
        v_part = head_view(values_all, index, block, depth)
        scores = (
            jnp.einsum("rhe,khe->hrk", q_part, k_part, preferred_element_type=jnp.float32) * scale
        )
        weights = jax.nn.softmax(scores, axis=-1).astype(jnp.bfloat16)
        mixed_part = jnp.einsum("hrk,khe->rhe", weights, v_part, preferred_element_type=jnp.float32)
        return mixed_part.reshape(count, block * depth)

    mixed = regroup(lax.map(forward_group, jnp.arange(groups))).astype(jnp.bfloat16)
    moved, finish_pull = jax.vjp(
        lambda inputs, mix: finish(inputs, mix, out_one), source_rows, mixed
    )
    curve_size = lax.axis_size("curve")
    capacity = 2 * count // curve_size
    target = hilbert_pos.reshape(count)
    owner = target // count
    offset = target % count
    columns = jnp.arange(curve_size, dtype=jnp.int32)
    onehot = (owner[:, None] == columns[None, :]).astype(jnp.bfloat16)
    earlier = (
        lax.broadcasted_iota(jnp.int32, (count, count), 0)
        > lax.broadcasted_iota(jnp.int32, (count, count), 1)
    ).astype(jnp.bfloat16)
    before = jnp.dot(earlier, onehot, preferred_element_type=jnp.float32)
    ranking = jnp.sum(before * onehot.astype(jnp.float32), axis=1).astype(jnp.int32)
    slot = owner * capacity + ranking
    outgoing = jnp.zeros((curve_size * capacity, width), jnp.bfloat16).at[slot].set(moved)
    outgoing_at = jnp.full((curve_size * capacity,), count, jnp.int32).at[slot].set(offset)
    arrived, arrived_at = (
        lax.all_to_all(
            outgoing.reshape(curve_size, capacity, width),
            "curve",
            split_axis=0,
            concat_axis=0,
            tiled=True,
        ),
        lax.all_to_all(
            outgoing_at.reshape(curve_size, capacity),
            "curve",
            split_axis=0,
            concat_axis=0,
            tiled=True,
        ),
    )
    landing = arrived_at.reshape(-1)
    hilbert_rows = (
        jnp.zeros((count, width), jnp.bfloat16)
        .at[landing]
        .set(arrived.reshape(-1, width), mode="drop")
    )
    segment = hilbert_seg.reshape(count)
    _, second_pull = jax.vjp(
        lambda inputs: device_block(inputs, segment, norm_gain_two, qkv_two, out_two), hilbert_rows
    )
    (hilbert_grad,) = second_pull(out_grad.reshape(count, width))
    valid = landing < count
    clipped = jnp.minimum(landing, count - 1)
    returning = jnp.where(
        valid[:, None], jnp.take(hilbert_grad, clipped, axis=0), jnp.zeros((), jnp.bfloat16)
    )
    arrived_home = lax.all_to_all(
        returning.reshape(curve_size, capacity, width),
        "curve",
        split_axis=0,
        concat_axis=0,
        tiled=True,
    )
    moved_grad = arrived_home.reshape(-1, width)[slot]
    residual_grad, mixed_grad = finish_pull(moved_grad)

    def backward_group(index):
        q_part = head_view(queries, index, block, depth)
        k_part = head_view(keys_all, index, block, depth)
        v_part = head_view(values_all, index, block, depth)
        g_part = head_view(mixed_grad, index, block, depth)
        scores = (
            jnp.einsum("rhe,khe->hrk", q_part, k_part, preferred_element_type=jnp.float32) * scale
        )
        weights = jax.nn.softmax(scores, axis=-1)
        rounded = weights.astype(jnp.bfloat16)
        weight_grad = round_trip(
            jnp.einsum("rhe,khe->hrk", g_part, v_part, preferred_element_type=jnp.float32)
        )
        score_grad = (
            weights * (weight_grad - jnp.sum(weights * weight_grad, axis=-1, keepdims=True)) * scale
        )
        query_grad = jnp.einsum("hrk,khe->rhe", score_grad, k_part.astype(jnp.float32)).reshape(
            count, block * depth
        )
        key_grad = jnp.einsum("hrk,rhe->khe", score_grad, q_part.astype(jnp.float32)).reshape(
            patch_len, block * depth
        )
        value_grad = jnp.einsum(
            "hrk,rhe->khe", rounded, g_part, preferred_element_type=jnp.float32
        ).reshape(patch_len, block * depth)
        return (query_grad, key_grad, value_grad)

    query_parts, key_parts, value_parts = lax.map(backward_group, jnp.arange(groups))
    query_grad = regroup(query_parts).astype(jnp.bfloat16)
    key_sum, value_sum = (
        lax.psum_scatter(regroup(key_parts), "patch", scatter_dimension=0, tiled=True),
        lax.psum_scatter(regroup(value_parts), "patch", scatter_dimension=0, tiled=True),
    )
    key_grad = key_sum.astype(jnp.bfloat16)
    value_grad = value_sum.astype(jnp.bfloat16)
    packed_grad = jnp.concatenate([query_grad, key_grad, value_grad], axis=1)
    (path_grad,) = prep_pull(packed_grad)
    total_grad = residual_grad + path_grad
    return total_grad.reshape(points.shape)


def solution(mesh):
    in_specs = (
        P("curve", "patch", None, None),
        P(),
        P(),
        P(),
        P("curve", "patch", None),
        P(),
        P(),
        P(),
        P("patch", "curve", None),
        P("patch", "curve", None, None),
    )
    out_specs = P("curve", "patch", None, None)
    return jax.shard_map(shards, mesh=mesh, in_specs=in_specs, out_specs=out_specs, check_vma=False)
```

profile of v0, /device:TPU:1, one launch (start us, length us, event | category | flops | bytes accessed | tf_op | source)
XLA Modules:
  0.0 356.9 jit_solution(2144473138300720519)
XLA Ops:
  9.0 2.1 convolution_convert_fusion.2
  14.4 18.4 %all-to-all-start = ((s32[128,1,4]{2,1,0:T(1,128)}), s32[128,1,4]{2,1,0:T(1,128)S(1)}, u32[]{:S(2)}, u32[]{:S(2)}) async-start(s32[128,1,4]{2,1,0:T(1,128)} %bitcast.21), calls=%async_computation | async-start | bytes 131072 | tf_op jit(solution)/shard_map/all_to_all | solution.py:126
  34.7 19.1 %all-gather.2.cloned.1.call-done = bf16[1024,1024]{1,0:T(8,128)(2,1)} async-done(((bf16[256,1024]{1,0:T(8,128)(2,1)}), bf16[1024,1024]{1,0:T(8,128)(2,1)}) %all-gather.2.cloned.1.call-update) | async-done | bytes 2097168 | tf_op jit(solution)/shard_map/all_gather | solution.py:82
  53.8 3.0 fusion.100
  56.8 1.5 copy.81
  58.3 2.3 copy.83
  61.3 40.3 %while.24 = (s32[]{:T(128)}, bf16[4,256,128]{1,2,0:T(8,128)(2,1)}, s32[4]{0:T(128)S(1)}, bf16[1024,512]{0,1:T(8,128)(2,1)S(1)}, bf16[256,512]{0,1:T(8,128)(2,1)}...) while((s32[]{:T(128)}, bf16[4,256,128]{1,2,0:T(8,128)(2,1)}, ...), condition=%wide.region_6.7_spmd, body=%wide.region_3.6_spmd.sunk | while | flops 139461632 | bytes 10363059 | solution.py:98
  64.4 3.4 fusion.159
  67.7 3.0 fusion.160
  74.5 3.4 fusion.159
  77.8 3.0 fusion.160
  84.5 3.4 fusion.159
  87.9 3.0 fusion.160
  94.6 3.4 fusion.159
  98.0 3.0 fusion.160
  101.6 2.1 fusion.43
  103.8 2.1 scatter_custom_fusion.1
  106.8 14.7 %all-to-all-start.1 = ((bf16[128,4,512]{2,1,0:T(4,128)(2,1)}), bf16[128,4,512]{2,1,0:T(4,128)(2,1)}, u32[]{:S(2)}, u32[]{:S(2)}) async-start(bf16[128,4,512]{2,1,0:T(4,128)(2,1)} %reshape.360), calls=%async_computation.1 | async-start | bytes 1048576 | tf_op jit(solution)/shard_map/all_to_all | solution.py:119
  125.1 16.6 %all-to-all-done.1 = bf16[128,4,512]{2,1,0:T(4,128)(2,1)} async-done(((bf16[128,4,512]{2,1,0:T(4,128)(2,1)}), bf16[128,4,512]{2,1,0:T(4,128)(2,1)}, u32[]{:S(2)}, u32[]{:S(2)}) %all-to-all-start.1) | async-done | bytes 524320 | tf_op jit(solution)/shard_map/all_to_all | solution.py:119
  141.8 2.0 reshape.406
  143.8 2.9 scatter_custom_fusion.2
  148.4 1.8 copy.85
  150.1 1.8 copy.84
  151.9 1.8 copy.87
  153.7 3.0 convolution_convert_fusion.3
  156.8 4.5 %fusion.102 = (f32[16,256]{1,0:T(8,128)S(1)}, f32[16,256,256]{1,2,0:T(8,128)}) fusion(pred[256,256]{0,1:T(8,128)(4,1)} %broadcast_compare_fusion, bf16[256,16,32]{0,2,1:T(8,128)(2,1)} %bitcast.185, bf16[256,16,32]{0,2,1:T(8,128)(2,1)} %bitcast.187), kind=kOutput, calls=%fused_computation.171 | convolution fusion | flops 71303424 | bytes 4800512 | tf_op jit(solution)/shard_map/jvp()/sub | solution.py:32
  161.3 4.0 %divide_convert_fusion.2 = (bf16[16,256,256]{1,2,0:T(8,128)(2,1)S(1)}, f32[16,256]{1,0:T(8,128)S(1)}) fusion(f32[16,256,256]{1,2,0:T(8,128)} %get-tuple-element.217, f32[16,256]{1,0:T(8,128)S(1)} %get-tuple-element.216, f32[16,256]{1,0:T(8,128)S(1)} %multiply_divide_fusion, bf16[16,256,256]{1,2,0:T(8,128)(2,1)} %convolution_convert_fusion.3), kind=kLoop, calls=%fused_computation.58 | loop fusion | flops 6287360 | bytes 8437760 | tf_op jit(solution)/shard_map/jvp()/convert_element_type | solution.py:33
  169.9 2.6 gather_fusion
  175.1 6.6 %all-to-all-start.2 = ((bf16[128,4,512]{2,1,0:T(4,128)(2,1)}), bf16[128,4,512]{2,1,0:T(4,128)(2,1)}, u32[]{:S(2)}, u32[]{:S(2)}) async-start(bf16[128,4,512]{2,1,0:T(4,128)(2,1)} %select_select_fusion), calls=%async_computation.2 | async-start | bytes 1048576 | tf_op jit(solution)/shard_map/all_to_all | solution.py:150
  181.8 19.7 %all-to-all-done.2 = bf16[128,4,512]{2,1,0:T(4,128)(2,1)} async-done(((bf16[128,4,512]{2,1,0:T(4,128)(2,1)}), bf16[128,4,512]{2,1,0:T(4,128)(2,1)}, u32[]{:S(2)}, u32[]{:S(2)}) %all-to-all-start.2) | async-done | bytes 524320 | tf_op jit(solution)/shard_map/all_to_all | solution.py:150
  202.6 1.9 gather_fusion.1
  204.5 2.1 convolution_convert_fusion.5
  207.3 74.5 %while.25 = (s32[]{:T(128)}, bf16[4,256,128]{1,2,0:T(8,128)(2,1)}, f32[4,1024,128]{1,2,0:T(8,128)}, f32[4,1024,128]{1,2,0:T(8,128)}, s32[4]{0:T(128)S(1)}, /*ind...) while((s32[]{:T(128)}, bf16[4,256,128]{1,2,0:T(8,128)(2,1)}, ...), condition=%wide.region_18.19_spmd, body=%wide.region_14.18_spmd.sunk | while | flops 356515840 | bytes 60391696 | solution.py:187
  210.5 2.1 convolution_convert_fusion.12
  213.4 3.4 fusion.171
  216.8 3.7 %fusion.172 = f32[4,256]{1,0:T(4,128)S(1)} fusion(bf16[4,256,1024]{2,1,0:T(8,128)(2,1)} %convolution_convert_fusion.12, f32[4,256,1024]{2,1,0:T(8,128)} %get-tuple-element.326, f32[4,256]{1,0:T(4,128)S(1)} %get-tuple-element.327), kind=kLoop, calls=%fused_computation.21.clone.1 | loop fusion | flops 4193280 | bytes 6299648 | tf_op jit(solution)/shard_map/while/body/eval_jaxpr/reduce_sum | solution.py:174
  229.1 2.1 convolution_convert_fusion.12
  232.1 3.3 fusion.171
  235.4 3.7 %fusion.172 = f32[4,256]{1,0:T(4,128)S(1)} fusion(bf16[4,256,1024]{2,1,0:T(8,128)(2,1)} %convolution_convert_fusion.12, f32[4,256,1024]{2,1,0:T(8,128)} %get-tuple-element.326, f32[4,256]{1,0:T(4,128)S(1)} %get-tuple-element.327), kind=kLoop, calls=%fused_computation.21.clone.1 | loop fusion | flops 4193280 | bytes 6299648 | tf_op jit(solution)/shard_map/while/body/eval_jaxpr/reduce_sum | solution.py:174
  247.7 2.1 convolution_convert_fusion.12
  250.7 3.4 fusion.171
  254.0 3.7 %fusion.172 = f32[4,256]{1,0:T(4,128)S(1)} fusion(bf16[4,256,1024]{2,1,0:T(8,128)(2,1)} %convolution_convert_fusion.12, f32[4,256,1024]{2,1,0:T(8,128)} %get-tuple-element.326, f32[4,256]{1,0:T(4,128)S(1)} %get-tuple-element.327), kind=kLoop, calls=%fused_computation.21.clone.1 | loop fusion | flops 4193280 | bytes 6299648 | tf_op jit(solution)/shard_map/while/body/eval_jaxpr/reduce_sum | solution.py:174
  266.3 2.1 convolution_convert_fusion.12
  269.3 3.4 fusion.171
  272.6 3.7 %fusion.172 = f32[4,256]{1,0:T(4,128)S(1)} fusion(bf16[4,256,1024]{2,1,0:T(8,128)(2,1)} %convolution_convert_fusion.12, f32[4,256,1024]{2,1,0:T(8,128)} %get-tuple-element.326, f32[4,256]{1,0:T(4,128)S(1)} %get-tuple-element.327), kind=kLoop, calls=%fused_computation.21.clone.1 | loop fusion | flops 4193280 | bytes 6299648 | tf_op jit(solution)/shard_map/while/body/eval_jaxpr/reduce_sum | solution.py:174
  282.6 25.7 %reduce-scatter.5.cloned.1.call-done = f32[256,512]{0,1:T(8,128)} async-done(((f32[1024,512]{0,1:T(8,128)}), f32[256,512]{0,1:T(8,128)}) %reduce-scatter.5.cloned.1.call-update) | async-done | bytes 524304 | tf_op jit(solution)/shard_map/reduce_scatter | solution.py:191
  309.4 36.8 %reduce-scatter.3.cloned.1.call-done = f32[256,512]{0,1:T(8,128)} async-done(((f32[1024,512]{0,1:T(8,128)}), f32[256,512]{0,1:T(8,128)}) %reduce-scatter.3.cloned.1.call-update) | async-done | bytes 524304 | tf_op jit(solution)/shard_map/reduce_scatter | solution.py:190
  347.3 2.1 fusion.68
  (173 shorter events, 75.0 us)
Async XLA Ops:
  6.5 140.3 %copy-start = (bf16[512,1536]{1,0:T(8,128)(2,1)S(1)}, bf16[512,1536]{1,0:T(8,128)(2,1)}, u32[]{:S(2)}) copy-start(bf16[512,1536]{1,0:T(8,128)(2,1)} %param.20) | copy-start | bytes 4718596
  6.5 5.5 %copy-start.18 = (s32[1,1,256]{2,1,0:T(1,128)S(1)}, s32[1,1,256]{2,1,0:T(1,128)}, u32[]{:S(2)}) copy-start(s32[1,1,256]{2,1,0:T(1,128)} %param.18) | copy-start | bytes 3076
  6.5 27.2 %copy-start.9 = (bf16[512,512]{1,0:T(8,128)(2,1)S(1)}, bf16[512,512]{1,0:T(8,128)(2,1)}, u32[]{:S(2)}) copy-start(bf16[512,512]{1,0:T(8,128)(2,1)} %param.21) | copy-start | bytes 1572868
  6.5 27.2 %copy-start.7 = (bf16[1,1,256,512]{3,2,1,0:T(8,128)(2,1)S(1)}, bf16[1,1,256,512]{3,2,1,0:T(8,128)(2,1)}, u32[]{:S(2)}) copy-start(bf16[1,1,256,512]{3,2,1,0:T(8,128)(2,1)} %param.23) | copy-start | bytes 786436
  6.5 47.3 %all-gather.2.cloned.1.call-start = ((), (), s32[]{:S(2)}) async-start(), calls=%async_computation.5 | async-start | bytes 2621440 | tf_op jit(solution)/shard_map/all_gather | solution.py:82
  7.8 0.6 copy-start.16
  8.4 0.6 copy-start.14
  14.4 92.4 %all-to-all-start = ((s32[128,1,4]{2,1,0:T(1,128)}), s32[128,1,4]{2,1,0:T(1,128)S(1)}, u32[]{:S(2)}, u32[]{:S(2)}) async-start(s32[128,1,4]{2,1,0:T(1,128)} %bitcast.21), calls=%async_computation | async-start | bytes 131072 | tf_op jit(solution)/shard_map/all_to_all | solution.py:126
  61.3 40.4 %copy-start.5 = (bf16[1,1,256,512]{3,2,1,0:T(8,128)(2,1)S(1)}, bf16[1,1,256,512]{3,2,1,0:T(8,128)(2,1)}, u32[]{:S(2)}) copy-start(bf16[1,1,256,512]{3,2,1,0:T(8,128)(2,1)} %param.14) | copy-start | bytes 786436
  61.3 60.3 %copy-start.19 = (s32[1,1,256]{2,1,0:T(1,128)S(1)}, s32[1,1,256]{2,1,0:T(1,128)}, u32[]{:S(2)}) copy-start(s32[1,1,256]{2,1,0:T(1,128)} %param.22) | copy-start | bytes 3076
  101.6 45.2 %copy-start.20 = (f32[512]{0:T(512)S(1)}, f32[512]{0:T(512)}, u32[]{:S(2)}) copy-start(f32[512]{0:T(512)} %param.19) | copy-start | bytes 6148
  106.8 35.0 %all-to-all-start.1 = ((bf16[128,4,512]{2,1,0:T(4,128)(2,1)}), bf16[128,4,512]{2,1,0:T(4,128)(2,1)}, u32[]{:S(2)}, u32[]{:S(2)}) async-start(bf16[128,4,512]{2,1,0:T(4,128)(2,1)} %reshape.360), calls=%async_computation.1 | async-start | bytes 1048576 | tf_op jit(solution)/shard_map/all_to_all | solution.py:119
  161.2 4.0 %copy-start.3 = (bf16[16,256,256]{1,2,0:T(8,128)(2,1)S(1)}, bf16[16,256,256]{1,2,0:T(8,128)(2,1)}, u32[]{:S(2)}) copy-start(bf16[16,256,256]{1,2,0:T(8,128)(2,1)} %convolution_convert_fusion.3) | copy-start | bytes 6291460
  161.2 4.7 %copy-start.4 = (f32[16,256,256]{1,2,0:T(8,128)S(1)}, f32[16,256,256]{1,2,0:T(8,128)}, u32[]{:S(2)}) copy-start(f32[16,256,256]{1,2,0:T(8,128)} %get-tuple-element.217) | copy-start | bytes 12582916
  161.3 4.7 %copy-start.11 = (bf16[256,512]{0,1:T(8,128)(2,1)S(1)}, bf16[256,512]{0,1:T(8,128)(2,1)}, u32[]{:S(2)}) copy-start(bf16[256,512]{0,1:T(8,128)(2,1)} %copy.85) | copy-start | bytes 786436
  161.3 4.7 %copy-start.13 = (pred[256,256]{0,1:T(8,128)(4,1)S(1)}, pred[256,256]{0,1:T(8,128)(4,1)}, u32[]{:S(2)}) copy-start(pred[256,256]{0,1:T(8,128)(4,1)} %broadcast_compare_fusion) | copy-start | bytes 196612
  165.9 1.2 copy-start.10
  168.3 1.5 copy-start.8
  175.1 26.4 %all-to-all-start.2 = ((bf16[128,4,512]{2,1,0:T(4,128)(2,1)}), bf16[128,4,512]{2,1,0:T(4,128)(2,1)}, u32[]{:S(2)}, u32[]{:S(2)}) async-start(bf16[128,4,512]{2,1,0:T(4,128)(2,1)} %select_select_fusion), calls=%async_computation.2 | async-start | bytes 1048576 | tf_op jit(solution)/shard_map/all_to_all | solution.py:150
  181.7 126.6 %reduce-scatter.5.cloned.1.call-start = ((), (), s32[]{:S(2)}) async-start(), calls=%async_computation.7 | async-start | bytes 2621440 | tf_op jit(solution)/shard_map/reduce_scatter | solution.py:191
  216.8 3.7 %copy-start.1 = (bf16[4,256,1024]{2,1,0:T(8,128)(2,1)S(1)}, bf16[4,256,1024]{2,1,0:T(8,128)(2,1)}, u32[]{:S(2)}) copy-start(bf16[4,256,1024]{2,1,0:T(8,128)(2,1)} %convolution_convert_fusion.12) | copy-start | bytes 6291460 | tf_op jit(solution)/shard_map/while
  216.8 4.7 %copy-start.2 = (f32[4,256,1024]{2,1,0:T(8,128)S(1)}, f32[4,256,1024]{2,1,0:T(8,128)}, u32[]{:S(2)}) copy-start(f32[4,256,1024]{2,1,0:T(8,128)} %get-tuple-element.326) | copy-start | bytes 12582916 | tf_op jit(solution)/shard_map/while
  235.4 3.7 %copy-start.1 = (bf16[4,256,1024]{2,1,0:T(8,128)(2,1)S(1)}, bf16[4,256,1024]{2,1,0:T(8,128)(2,1)}, u32[]{:S(2)}) copy-start(bf16[4,256,1024]{2,1,0:T(8,128)(2,1)} %convolution_convert_fusion.12) | copy-start | bytes 6291460 | tf_op jit(solution)/shard_map/while
  235.4 4.7 %copy-start.2 = (f32[4,256,1024]{2,1,0:T(8,128)S(1)}, f32[4,256,1024]{2,1,0:T(8,128)}, u32[]{:S(2)}) copy-start(f32[4,256,1024]{2,1,0:T(8,128)} %get-tuple-element.326) | copy-start | bytes 12582916 | tf_op jit(solution)/shard_map/while
  254.0 3.7 %copy-start.1 = (bf16[4,256,1024]{2,1,0:T(8,128)(2,1)S(1)}, bf16[4,256,1024]{2,1,0:T(8,128)(2,1)}, u32[]{:S(2)}) copy-start(bf16[4,256,1024]{2,1,0:T(8,128)(2,1)} %convolution_convert_fusion.12) | copy-start | bytes 6291460 | tf_op jit(solution)/shard_map/while
  254.0 4.7 %copy-start.2 = (f32[4,256,1024]{2,1,0:T(8,128)S(1)}, f32[4,256,1024]{2,1,0:T(8,128)}, u32[]{:S(2)}) copy-start(f32[4,256,1024]{2,1,0:T(8,128)} %get-tuple-element.326) | copy-start | bytes 12582916 | tf_op jit(solution)/shard_map/while
  272.6 3.7 %copy-start.1 = (bf16[4,256,1024]{2,1,0:T(8,128)(2,1)S(1)}, bf16[4,256,1024]{2,1,0:T(8,128)(2,1)}, u32[]{:S(2)}) copy-start(bf16[4,256,1024]{2,1,0:T(8,128)(2,1)} %convolution_convert_fusion.12) | copy-start | bytes 6291460 | tf_op jit(solution)/shard_map/while
  272.6 4.7 %copy-start.2 = (f32[4,256,1024]{2,1,0:T(8,128)S(1)}, f32[4,256,1024]{2,1,0:T(8,128)}, u32[]{:S(2)}) copy-start(f32[4,256,1024]{2,1,0:T(8,128)} %get-tuple-element.326) | copy-start | bytes 12582916 | tf_op jit(solution)/shard_map/while
  281.8 65.4 %copy-start.12 = (bf16[4,256,128]{1,2,0:T(8,128)(2,1)S(1)}, bf16[4,256,128]{1,2,0:T(8,128)(2,1)}, u32[]{:S(2)}) copy-start(bf16[4,256,128]{1,2,0:T(8,128)(2,1)} %get-tuple-element.87) | copy-start | bytes 786436
  281.8 65.4 %copy-start.21 = (f32[512]{0:T(512)S(1)}, f32[512]{0:T(512)}, u32[]{:S(2)}) copy-start(f32[512]{0:T(512)} %param.15) | copy-start | bytes 6148
  281.9 67.5 %copy-start.17 = (f32[256]{0:T(256)S(1)}, f32[256]{0:T(256)}, u32[]{:S(2)}) copy-start(f32[256]{0:T(256)} %copy-done.16) | copy-start | bytes 3076
  281.9 67.5 %copy-start.6 = (bf16[256,512]{1,0:T(8,128)(2,1)S(1)}, bf16[256,512]{1,0:T(8,128)(2,1)}, u32[]{:S(2)}) copy-start(bf16[256,512]{1,0:T(8,128)(2,1)} %gather_fusion.1) | copy-start | bytes 786436
  281.9 67.5 %copy-start.15 = (f32[256]{0:T(256)S(1)}, f32[256]{0:T(256)}, u32[]{:S(2)}) copy-start(f32[256]{0:T(256)} %copy-done.14) | copy-start | bytes 3076
  281.9 64.3 %reduce-scatter.3.cloned.1.call-start = ((), (), s32[]{:S(2)}) async-start(), calls=%async_computation.6 | async-start | bytes 2621440 | tf_op jit(solution)/shard_map/reduce_scatter | solution.py:190
Sparse Core Ops, SparseCore 0:
  12.1 41.6 all-gather.1
  282.0 26.2 reduce-scatter.4
  311.4 34.7 reduce-scatter.2
where the time goes:
time: 359 us; the launch traced here: 357 us
  waiting for transfers between devices  119 us (33%)
  matrix products  80.1 us (22%)
  local copies, waits for them, and re-layouts  73.3 us (20%)
  starting transfers between devices  39.9 us (11%)
  other arithmetic  26.5 us (7%)
  between operations  13.5 us (4%)
  loops' own time  5.05 us (1%)
    reduce_scatter x1, waiting for transfers between devices, shards(): lax.psum_scatter(regroup(key_parts), 'patch', scatter_dimension=0, tiled=...  36.8 us
    reduce_scatter x1, waiting for transfers between devices, shards(): lax.psum_scatter(regroup(value_parts), 'patch', scatter_dimension=0, tile...  25.7 us
    all_to_all x1, waiting for transfers between devices, shards(): lax.all_to_all(returning.reshape(curve_size, capacity, width), 'curve', s...  19.7 us
    all_gather x1, waiting for transfers between devices, shards(): gathered = lax.all_gather(packed[:, width:], 'patch', axis=0, tiled=True)  19.1 us
    dynamic_slice x28, local copies, waits for them, and re-layouts, head_view(): piece = lax.dynamic_slice_in_dim(matrix, index * columns, columns, 1)  18.6 us
    all_to_all x1, starting transfers between devices, shards(): lax.all_to_all(outgoing_at.reshape(curve_size, capacity), 'curve', split_...  18.4 us
    all_to_all x1, waiting for transfers between devices, shards(): lax.all_to_all(outgoing.reshape(curve_size, capacity, width), 'curve', sp...  16.6 us
    reduce_sum x4, other arithmetic, backward_group(): jnp.sum(weights * weight_grad, axis=-1, keepdims=True)  14.8 us
  transfers between devices with their start and end apart: 6, of which 5 were waited for; matrix products, arithmetic and copies ran while one was open for 16% of the time, Pallas kernels for 0%

commit v1 on v0

--- a/solution.py
+++ b/solution.py
@@ -79,7 +79,11 @@
     source_rows = points.reshape(count, width)
     packed, prep_pull = jax.vjp(lambda inputs: prepare(inputs, norm_gain_one, qkv_one), source_rows)
     queries = packed[:, :width]
-    gathered = lax.all_gather(packed[:, width:], "patch", axis=0, tiled=True)
+    x = packed[:, width:]
+    devices = lax.axis_size("patch")
+    blocks = jnp.stack([x for _ in range(devices)])
+    blocks = lax.all_to_all(blocks, "patch", split_axis=0, concat_axis=0)
+    gathered = jnp.concatenate(blocks, axis=0)
     keys_all = gathered[:, :width]
     values_all = gathered[:, width:]
     patch_len = gathered.shape[0]

time: 359 us -> 372 us (1.036)
  starting transfers between devices: 39.9 us -> 50.4 us
  local copies, waits for them, and re-layouts: 73.3 us -> 78.8 us
  waiting for transfers between devices: 119 us -> 115 us
    all_gather x1 -> x0, waiting for transfers between devices: 19.1 us -> none  [shards(): gathered = lax.all_gather(packed[:, width:], 'patch', axis=0, tiled=True)]
    all_to_all x0 -> x1, waiting for transfers between devices: none -> 15.8 us  [shards(): blocks = lax.all_to_all(blocks, 'patch', split_axis=0, concat_axis=0)]
    all_to_all x1, starting transfers between devices: 18.4 us -> 24.6 us  [shards(): lax.all_to_all(outgoing_at.reshape(curve_size, capacity), 'curve', split_...]
    all_to_all x0 -> x1, starting transfers between devices: none -> 4.97 us  [shards(): blocks = lax.all_to_all(blocks, 'patch', split_axis=0, concat_axis=0)]
    all_to_all x0 -> x1, local copies, waits for them, and re-layouts: none -> 3.98 us  [shards(): blocks = lax.all_to_all(blocks, 'patch', split_axis=0, concat_axis=0)]
  transfers between devices with their start and end apart: 6 -> 6, of which waited for: 5 -> 5; matrix products, arithmetic and copies ran while one was open for 16% -> 17% of each run, Pallas kernels for 0% -> 0%
where the time goes in v1:
time: 372 us; the launch traced here: 369 us
  waiting for transfers between devices  115 us (31%)
  matrix products  80.1 us (22%)
  local copies, waits for them, and re-layouts  78.8 us (21%)
  starting transfers between devices  50.4 us (14%)
  other arithmetic  26.4 us (7%)
  between operations  13.8 us (4%)
  loops' own time  5.05 us (1%)
    reduce_scatter x1, waiting for transfers between devices, shards(): lax.psum_scatter(regroup(key_parts), 'patch', scatter_dimension=0, tiled=...  36.8 us
    reduce_scatter x1, waiting for transfers between devices, shards(): lax.psum_scatter(regroup(value_parts), 'patch', scatter_dimension=0, tile...  25.1 us
    all_to_all x1, starting transfers between devices, shards(): lax.all_to_all(outgoing_at.reshape(curve_size, capacity), 'curve', split_...  24.6 us
    all_to_all x1, waiting for transfers between devices, shards(): lax.all_to_all(returning.reshape(curve_size, capacity, width), 'curve', s...  19.7 us
    dynamic_slice x28, local copies, waits for them, and re-layouts, head_view(): piece = lax.dynamic_slice_in_dim(matrix, index * columns, columns, 1)  18.6 us
    all_to_all x1, waiting for transfers between devices, shards(): lax.all_to_all(outgoing.reshape(curve_size, capacity, width), 'curve', sp...  16.6 us
    all_to_all x1, waiting for transfers between devices, shards(): blocks = lax.all_to_all(blocks, 'patch', split_axis=0, concat_axis=0)  15.8 us
    reduce_sum x4, other arithmetic, backward_group(): jnp.sum(weights * weight_grad, axis=-1, keepdims=True)  14.8 us
  transfers between devices with their start and end apart: 6, of which 5 were waited for; matrix products, arithmetic and copies ran while one was open for 17% of the time, Pallas kernels for 0%

profile of v1, /device:TPU:1, one launch (start us, length us, event | category | flops | bytes accessed | tf_op | source)
XLA Modules:
  0.0 369.4 jit_solution(11582776343853068389)
XLA Ops:
  7.8 2.1 convolution_convert_fusion.2
  13.5 5.0 %all-to-all-start.1 = ((bf16[4,256,1024]{1,2,0:T(8,128)(2,1)}), bf16[4,256,1024]{1,2,0:T(8,128)(2,1)}, u32[]{:S(2)}, u32[]{:S(2)}) async-start(bf16[4,256,1024]{1,2,0:T(8,128)(2,1)} %stack.2), calls=%async_computation.1 | async-start | bytes 4194304 | tf_op jit(solution)/shard_map/all_to_all | solution.py:85
  22.8 15.8 %all-to-all-done.1 = bf16[4,256,1024]{1,2,0:T(8,128)(2,1)} async-done(((bf16[4,256,1024]{1,2,0:T(8,128)(2,1)}), bf16[4,256,1024]{1,2,0:T(8,128)(2,1)}, u32[]{:S(2)}, u32[]{:S(2)}) %all-to-all-start.1) | async-done | bytes 2097184 | tf_op jit(solution)/shard_map/all_to_all | solution.py:85
  38.6 24.6 %all-to-all-start = ((s32[128,1,4]{2,1,0:T(1,128)}), s32[128,1,4]{2,1,0:T(1,128)S(1)}, u32[]{:S(2)}, u32[]{:S(2)}) async-start(s32[128,1,4]{2,1,0:T(1,128)} %bitcast.21), calls=%async_computation | async-start | bytes 131072 | tf_op jit(solution)/shard_map/all_to_all | solution.py:130
  63.2 4.0 %copy.75 = bf16[4,256,1024]{2,1,0:T(8,128)(2,1)} copy(bf16[4,256,1024]{1,2,0:T(8,128)(2,1)} %all-to-all-done.1) | data formatting | bytes 4194304 | tf_op jit(solution)/shard_map/all_to_all | solution.py:85
  67.1 3.0 fusion.100
  71.7 2.3 copy.78
  74.7 40.3 %while.24 = (s32[]{:T(128)}, bf16[4,256,128]{1,2,0:T(8,128)(2,1)}, s32[4]{0:T(128)S(1)}, bf16[1024,512]{0,1:T(8,128)(2,1)S(1)}, bf16[256,512]{0,1:T(8,128)(2,1)}...) while((s32[]{:T(128)}, bf16[4,256,128]{1,2,0:T(8,128)(2,1)}, ...), condition=%wide.region_6.7_spmd, body=%wide.region_3.6_spmd.sunk | while | flops 139461632 | bytes 10363059 | solution.py:102
  77.8 3.3 fusion.159
  81.1 3.0 fusion.160
  87.8 3.3 fusion.159
  91.2 3.0 fusion.160
  97.9 3.3 fusion.159
  101.3 3.0 fusion.160
  108.0 3.3 fusion.159
  111.3 3.0 fusion.160
  115.0 2.1 fusion.43
  117.1 2.1 scatter_custom_fusion.1
  120.2 14.2 %all-to-all-start.2 = ((bf16[128,4,512]{2,1,0:T(4,128)(2,1)}), bf16[128,4,512]{2,1,0:T(4,128)(2,1)}, u32[]{:S(2)}, u32[]{:S(2)}) async-start(bf16[128,4,512]{2,1,0:T(4,128)(2,1)} %reshape.366), calls=%async_computation.2 | async-start | bytes 1048576 | tf_op jit(solution)/shard_map/all_to_all | solution.py:123
  137.9 16.6 %all-to-all-done.2 = bf16[128,4,512]{2,1,0:T(4,128)(2,1)} async-done(((bf16[128,4,512]{2,1,0:T(4,128)(2,1)}), bf16[128,4,512]{2,1,0:T(4,128)(2,1)}, u32[]{:S(2)}, u32[]{:S(2)}) %all-to-all-start.2) | async-done | bytes 524320 | tf_op jit(solution)/shard_map/all_to_all | solution.py:123
  154.6 2.0 reshape.412
  156.6 2.9 scatter_custom_fusion.2
  161.2 1.8 copy.80
  164.7 1.8 copy.82
  166.6 3.0 convolution_convert_fusion.3
  169.6 4.5 %fusion.102 = (f32[16,256]{1,0:T(8,128)S(1)}, f32[16,256,256]{1,2,0:T(8,128)}) fusion(pred[256,256]{0,1:T(8,128)(4,1)} %broadcast_compare_fusion, bf16[256,16,32]{0,2,1:T(8,128)(2,1)} %bitcast.187, bf16[256,16,32]{0,2,1:T(8,128)(2,1)} %bitcast.189), kind=kOutput, calls=%fused_computation.171 | convolution fusion | flops 71303424 | bytes 4800512 | tf_op jit(solution)/shard_map/jvp()/sub | solution.py:32
  174.1 4.0 %divide_convert_fusion.2 = (bf16[16,256,256]{1,2,0:T(8,128)(2,1)S(1)}, f32[16,256]{1,0:T(8,128)S(1)}) fusion(f32[16,256,256]{1,2,0:T(8,128)} %get-tuple-element.217, f32[16,256]{1,0:T(8,128)S(1)} %get-tuple-element.216, f32[16,256]{1,0:T(8,128)S(1)} %multiply_divide_fusion, bf16[16,256,256]{1,2,0:T(8,128)(2,1)} %convolution_convert_fusion.3), kind=kLoop, calls=%fused_computation.58 | loop fusion | flops 6287360 | bytes 8437760 | tf_op jit(solution)/shard_map/jvp()/convert_element_type | solution.py:33
  182.7 2.6 gather_fusion
  187.9 6.6 %all-to-all-start.3 = ((bf16[128,4,512]{2,1,0:T(4,128)(2,1)}), bf16[128,4,512]{2,1,0:T(4,128)(2,1)}, u32[]{:S(2)}, u32[]{:S(2)}) async-start(bf16[128,4,512]{2,1,0:T(4,128)(2,1)} %select_select_fusion), calls=%async_computation.3 | async-start | bytes 1048576 | tf_op jit(solution)/shard_map/all_to_all | solution.py:154
  194.6 19.7 %all-to-all-done.3 = bf16[128,4,512]{2,1,0:T(4,128)(2,1)} async-done(((bf16[128,4,512]{2,1,0:T(4,128)(2,1)}), bf16[128,4,512]{2,1,0:T(4,128)(2,1)}, u32[]{:S(2)}, u32[]{:S(2)}) %all-to-all-start.3) | async-done | bytes 524320 | tf_op jit(solution)/shard_map/all_to_all | solution.py:154
  215.4 1.9 gather_fusion.1
  217.3 2.1 convolution_convert_fusion.5
  220.2 74.5 %while.25 = (s32[]{:T(128)}, bf16[4,256,128]{1,2,0:T(8,128)(2,1)}, f32[4,1024,128]{1,2,0:T(8,128)}, f32[4,1024,128]{1,2,0:T(8,128)}, s32[4]{0:T(128)S(1)}, /*ind...) while((s32[]{:T(128)}, bf16[4,256,128]{1,2,0:T(8,128)(2,1)}, ...), condition=%wide.region_18.19_spmd, body=%wide.region_14.18_spmd.sunk | while | flops 356515840 | bytes 60391696 | solution.py:191
  223.3 2.1 convolution_convert_fusion.12
  226.2 3.3 fusion.171
  229.6 3.7 %fusion.172 = f32[4,256]{1,0:T(4,128)S(1)} fusion(bf16[4,256,1024]{2,1,0:T(8,128)(2,1)} %convolution_convert_fusion.12, f32[4,256,1024]{2,1,0:T(8,128)} %get-tuple-element.326, f32[4,256]{1,0:T(4,128)S(1)} %get-tuple-element.327), kind=kLoop, calls=%fused_computation.21.clone.1 | loop fusion | flops 4193280 | bytes 6299648 | tf_op jit(solution)/shard_map/while/body/eval_jaxpr/reduce_sum | solution.py:178
  241.9 2.1 convolution_convert_fusion.12
  244.9 3.3 fusion.171
  248.2 3.7 %fusion.172 = f32[4,256]{1,0:T(4,128)S(1)} fusion(bf16[4,256,1024]{2,1,0:T(8,128)(2,1)} %convolution_convert_fusion.12, f32[4,256,1024]{2,1,0:T(8,128)} %get-tuple-element.326, f32[4,256]{1,0:T(4,128)S(1)} %get-tuple-element.327), kind=kLoop, calls=%fused_computation.21.clone.1 | loop fusion | flops 4193280 | bytes 6299648 | tf_op jit(solution)/shard_map/while/body/eval_jaxpr/reduce_sum | solution.py:178
  260.5 2.1 convolution_convert_fusion.12
  263.5 3.3 fusion.171
  266.8 3.7 %fusion.172 = f32[4,256]{1,0:T(4,128)S(1)} fusion(bf16[4,256,1024]{2,1,0:T(8,128)(2,1)} %convolution_convert_fusion.12, f32[4,256,1024]{2,1,0:T(8,128)} %get-tuple-element.326, f32[4,256]{1,0:T(4,128)S(1)} %get-tuple-element.327), kind=kLoop, calls=%fused_computation.21.clone.1 | loop fusion | flops 4193280 | bytes 6299648 | tf_op jit(solution)/shard_map/while/body/eval_jaxpr/reduce_sum | solution.py:178
  279.1 2.1 convolution_convert_fusion.12
  282.1 3.4 fusion.171
  285.4 3.7 %fusion.172 = f32[4,256]{1,0:T(4,128)S(1)} fusion(bf16[4,256,1024]{2,1,0:T(8,128)(2,1)} %convolution_convert_fusion.12, f32[4,256,1024]{2,1,0:T(8,128)} %get-tuple-element.326, f32[4,256]{1,0:T(4,128)S(1)} %get-tuple-element.327), kind=kLoop, calls=%fused_computation.21.clone.1 | loop fusion | flops 4193280 | bytes 6299648 | tf_op jit(solution)/shard_map/while/body/eval_jaxpr/reduce_sum | solution.py:178
  295.4 25.1 %reduce-scatter.5.cloned.1.call-done = f32[256,512]{0,1:T(8,128)} async-done(((f32[1024,512]{0,1:T(8,128)}), f32[256,512]{0,1:T(8,128)}) %reduce-scatter.5.cloned.1.call-update) | async-done | bytes 524304 | tf_op jit(solution)/shard_map/reduce_scatter | solution.py:195
  321.6 36.8 %reduce-scatter.3.cloned.1.call-done = f32[256,512]{0,1:T(8,128)} async-done(((f32[1024,512]{0,1:T(8,128)}), f32[256,512]{0,1:T(8,128)}) %reduce-scatter.3.cloned.1.call-update) | async-done | bytes 524304 | tf_op jit(solution)/shard_map/reduce_scatter | solution.py:194
  359.5 2.1 fusion.68
  (175 shorter events, 79.7 us)
Async XLA Ops:
  6.5 153.1 %copy-start = (bf16[512,1536]{1,0:T(8,128)(2,1)S(1)}, bf16[512,1536]{1,0:T(8,128)(2,1)}, u32[]{:S(2)}) copy-start(bf16[512,1536]{1,0:T(8,128)(2,1)} %param.20) | copy-start | bytes 4718596
  7.7 3.0 copy-start.16
  7.8 3.0 copy-start.14
  10.8 7.7 %copy-start.18 = (s32[1,1,256]{2,1,0:T(1,128)S(1)}, s32[1,1,256]{2,1,0:T(1,128)}, u32[]{:S(2)}) copy-start(s32[1,1,256]{2,1,0:T(1,128)} %param.18) | copy-start | bytes 3076
  12.0 9.7 %copy-start.7 = (bf16[1,1,256,512]{3,2,1,0:T(8,128)(2,1)S(1)}, bf16[1,1,256,512]{3,2,1,0:T(8,128)(2,1)}, u32[]{:S(2)}) copy-start(bf16[1,1,256,512]{3,2,1,0:T(8,128)(2,1)} %param.23) | copy-start | bytes 786436
  13.5 8.3 %copy-start.9 = (bf16[512,512]{1,0:T(8,128)(2,1)S(1)}, bf16[512,512]{1,0:T(8,128)(2,1)}, u32[]{:S(2)}) copy-start(bf16[512,512]{1,0:T(8,128)(2,1)} %param.21) | copy-start | bytes 1572868
  13.5 25.1 %all-to-all-start.1 = ((bf16[4,256,1024]{1,2,0:T(8,128)(2,1)}), bf16[4,256,1024]{1,2,0:T(8,128)(2,1)}, u32[]{:S(2)}, u32[]{:S(2)}) async-start(bf16[4,256,1024]{1,2,0:T(8,128)(2,1)} %stack.2), calls=%async_computation.1 | async-start | bytes 4194304 | tf_op jit(solution)/shard_map/all_to_all | solution.py:85
  38.6 81.6 %all-to-all-start = ((s32[128,1,4]{2,1,0:T(1,128)}), s32[128,1,4]{2,1,0:T(1,128)S(1)}, u32[]{:S(2)}, u32[]{:S(2)}) async-start(s32[128,1,4]{2,1,0:T(1,128)} %bitcast.21), calls=%async_computation | async-start | bytes 131072 | tf_op jit(solution)/shard_map/all_to_all | solution.py:130
  74.7 40.3 %copy-start.5 = (bf16[1,1,256,512]{3,2,1,0:T(8,128)(2,1)S(1)}, bf16[1,1,256,512]{3,2,1,0:T(8,128)(2,1)}, u32[]{:S(2)}) copy-start(bf16[1,1,256,512]{3,2,1,0:T(8,128)(2,1)} %param.14) | copy-start | bytes 786436
  74.7 59.7 %copy-start.19 = (s32[1,1,256]{2,1,0:T(1,128)S(1)}, s32[1,1,256]{2,1,0:T(1,128)}, u32[]{:S(2)}) copy-start(s32[1,1,256]{2,1,0:T(1,128)} %param.22) | copy-start | bytes 3076
  115.0 44.6 %copy-start.20 = (f32[512]{0:T(512)S(1)}, f32[512]{0:T(512)}, u32[]{:S(2)}) copy-start(f32[512]{0:T(512)} %param.19) | copy-start | bytes 6148
  120.2 34.4 %all-to-all-start.2 = ((bf16[128,4,512]{2,1,0:T(4,128)(2,1)}), bf16[128,4,512]{2,1,0:T(4,128)(2,1)}, u32[]{:S(2)}, u32[]{:S(2)}) async-start(bf16[128,4,512]{2,1,0:T(4,128)(2,1)} %reshape.366), calls=%async_computation.2 | async-start | bytes 1048576 | tf_op jit(solution)/shard_map/all_to_all | solution.py:123
  174.0 4.0 %copy-start.3 = (bf16[16,256,256]{1,2,0:T(8,128)(2,1)S(1)}, bf16[16,256,256]{1,2,0:T(8,128)(2,1)}, u32[]{:S(2)}) copy-start(bf16[16,256,256]{1,2,0:T(8,128)(2,1)} %convolution_convert_fusion.3) | copy-start | bytes 6291460
  174.1 4.7 %copy-start.4 = (f32[16,256,256]{1,2,0:T(8,128)S(1)}, f32[16,256,256]{1,2,0:T(8,128)}, u32[]{:S(2)}) copy-start(f32[16,256,256]{1,2,0:T(8,128)} %get-tuple-element.217) | copy-start | bytes 12582916
  174.1 4.7 %copy-start.11 = (bf16[256,512]{0,1:T(8,128)(2,1)S(1)}, bf16[256,512]{0,1:T(8,128)(2,1)}, u32[]{:S(2)}) copy-start(bf16[256,512]{0,1:T(8,128)(2,1)} %copy.80) | copy-start | bytes 786436
  174.1 4.7 %copy-start.13 = (pred[256,256]{0,1:T(8,128)(4,1)S(1)}, pred[256,256]{0,1:T(8,128)(4,1)}, u32[]{:S(2)}) copy-start(pred[256,256]{0,1:T(8,128)(4,1)} %broadcast_compare_fusion) | copy-start | bytes 196612
  178.7 1.2 copy-start.10
  181.1 1.5 copy-start.8
  187.9 26.4 %all-to-all-start.3 = ((bf16[128,4,512]{2,1,0:T(4,128)(2,1)}), bf16[128,4,512]{2,1,0:T(4,128)(2,1)}, u32[]{:S(2)}, u32[]{:S(2)}) async-start(bf16[128,4,512]{2,1,0:T(4,128)(2,1)} %select_select_fusion), calls=%async_computation.3 | async-start | bytes 1048576 | tf_op jit(solution)/shard_map/all_to_all | solution.py:154
  194.5 126.0 %reduce-scatter.5.cloned.1.call-start = ((), (), s32[]{:S(2)}) async-start(), calls=%async_computation.7 | async-start | bytes 2621440 | tf_op jit(solution)/shard_map/reduce_scatter | solution.py:195
  229.6 3.7 %copy-start.1 = (bf16[4,256,1024]{2,1,0:T(8,128)(2,1)S(1)}, bf16[4,256,1024]{2,1,0:T(8,128)(2,1)}, u32[]{:S(2)}) copy-start(bf16[4,256,1024]{2,1,0:T(8,128)(2,1)} %convolution_convert_fusion.12) | copy-start | bytes 6291460 | tf_op jit(solution)/shard_map/while
  229.6 4.7 %copy-start.2 = (f32[4,256,1024]{2,1,0:T(8,128)S(1)}, f32[4,256,1024]{2,1,0:T(8,128)}, u32[]{:S(2)}) copy-start(f32[4,256,1024]{2,1,0:T(8,128)} %get-tuple-element.326) | copy-start | bytes 12582916 | tf_op jit(solution)/shard_map/while
  248.2 3.7 %copy-start.1 = (bf16[4,256,1024]{2,1,0:T(8,128)(2,1)S(1)}, bf16[4,256,1024]{2,1,0:T(8,128)(2,1)}, u32[]{:S(2)}) copy-start(bf16[4,256,1024]{2,1,0:T(8,128)(2,1)} %convolution_convert_fusion.12) | copy-start | bytes 6291460 | tf_op jit(solution)/shard_map/while
  248.2 4.7 %copy-start.2 = (f32[4,256,1024]{2,1,0:T(8,128)S(1)}, f32[4,256,1024]{2,1,0:T(8,128)}, u32[]{:S(2)}) copy-start(f32[4,256,1024]{2,1,0:T(8,128)} %get-tuple-element.326) | copy-start | bytes 12582916 | tf_op jit(solution)/shard_map/while
  266.8 3.7 %copy-start.1 = (bf16[4,256,1024]{2,1,0:T(8,128)(2,1)S(1)}, bf16[4,256,1024]{2,1,0:T(8,128)(2,1)}, u32[]{:S(2)}) copy-start(bf16[4,256,1024]{2,1,0:T(8,128)(2,1)} %convolution_convert_fusion.12) | copy-start | bytes 6291460 | tf_op jit(solution)/shard_map/while
  266.8 4.7 %copy-start.2 = (f32[4,256,1024]{2,1,0:T(8,128)S(1)}, f32[4,256,1024]{2,1,0:T(8,128)}, u32[]{:S(2)}) copy-start(f32[4,256,1024]{2,1,0:T(8,128)} %get-tuple-element.326) | copy-start | bytes 12582916 | tf_op jit(solution)/shard_map/while
  285.4 3.7 %copy-start.1 = (bf16[4,256,1024]{2,1,0:T(8,128)(2,1)S(1)}, bf16[4,256,1024]{2,1,0:T(8,128)(2,1)}, u32[]{:S(2)}) copy-start(bf16[4,256,1024]{2,1,0:T(8,128)(2,1)} %convolution_convert_fusion.12) | copy-start | bytes 6291460 | tf_op jit(solution)/shard_map/while
  285.4 4.7 %copy-start.2 = (f32[4,256,1024]{2,1,0:T(8,128)S(1)}, f32[4,256,1024]{2,1,0:T(8,128)}, u32[]{:S(2)}) copy-start(f32[4,256,1024]{2,1,0:T(8,128)} %get-tuple-element.326) | copy-start | bytes 12582916 | tf_op jit(solution)/shard_map/while
  294.6 64.9 %copy-start.12 = (bf16[4,256,128]{1,2,0:T(8,128)(2,1)S(1)}, bf16[4,256,128]{1,2,0:T(8,128)(2,1)}, u32[]{:S(2)}) copy-start(bf16[4,256,128]{1,2,0:T(8,128)(2,1)} %get-tuple-element.87) | copy-start | bytes 786436
  294.6 64.9 %copy-start.21 = (f32[512]{0:T(512)S(1)}, f32[512]{0:T(512)}, u32[]{:S(2)}) copy-start(f32[512]{0:T(512)} %param.15) | copy-start | bytes 6148
  294.7 66.9 %copy-start.17 = (f32[256]{0:T(256)S(1)}, f32[256]{0:T(256)}, u32[]{:S(2)}) copy-start(f32[256]{0:T(256)} %copy-done.16) | copy-start | bytes 3076
  294.7 67.0 %copy-start.6 = (bf16[256,512]{1,0:T(8,128)(2,1)S(1)}, bf16[256,512]{1,0:T(8,128)(2,1)}, u32[]{:S(2)}) copy-start(bf16[256,512]{1,0:T(8,128)(2,1)} %gather_fusion.1) | copy-start | bytes 786436
  294.7 67.0 %copy-start.15 = (f32[256]{0:T(256)S(1)}, f32[256]{0:T(256)}, u32[]{:S(2)}) copy-start(f32[256]{0:T(256)} %copy-done.14) | copy-start | bytes 3076
  294.7 63.7 %reduce-scatter.3.cloned.1.call-start = ((), (), s32[]{:S(2)}) async-start(), calls=%async_computation.6 | async-start | bytes 2621440 | tf_op jit(solution)/shard_map/reduce_scatter | solution.py:194
Sparse Core Ops, SparseCore 0:
  294.8 25.6 reduce-scatter.4
  323.6 34.7 reduce-scatter.2
